TPU v7x, 256 devices: a whole 4x4x8 slice. The times are simulated.
256 devices in a mesh: dp: 4 (over y_hi, core), fsdp: 64 (over z, y_lo, x).
Axes of the slice: x: 4, y: 4 (y_hi: 2, y_lo: 2; y = y_hi * 2 + y_lo), z: 8, core: 2. Of those that a mesh axis runs over, the one named last changes fastest.
Arguments:
- inputs: bfloat16 [256, 512, 768], P(('dp', 'fsdp')), may hold values from -6 to 6
- segment_ids: int32 [256, 512], P(('dp', 'fsdp')), may hold values from 0 to 3, never falling along the last dimension, each value on 1 to 256 neighbouring positions
- cotangent: bfloat16 [256, 512, 768], P(('dp', 'fsdp')), may hold values from -24 to 24
- qkv_weight: bfloat16 [768, 2304], P('fsdp'), may hold values from -0.21875 to 0.21875
- query_bias: bfloat16 [768], P('fsdp'), may hold values from -3 to 3
- value_bias: bfloat16 [768], P('fsdp'), may hold values from -0.59765625 to 0.59765625
- out_weight: bfloat16 [768, 768], P('fsdp'), may hold values from -2.5 to 2.5
- out_bias: bfloat16 [768], P('fsdp'), may hold values from -1.1953125 to 1.1953125
- attn_gain: bfloat16 [768], P('fsdp'), may hold values from 0.25 to 1.75
- attn_shift: bfloat16 [768], P('fsdp'), may hold values from -1.1953125 to 1.1953125
- up_weight: bfloat16 [768, 3072], P('fsdp'), may hold values from -0.21875 to 0.21875
- up_bias: bfloat16 [3072], P('fsdp'), may hold values from -1.796875 to 1.796875
- down_weight: bfloat16 [3072, 768], P('fsdp'), may hold values from -0.15625 to 0.15625
- down_bias: bfloat16 [768], P('fsdp'), may hold values from -1.1953125 to 1.1953125
- ffn_gain: bfloat16 [768], P('fsdp'), may hold values from 0.25 to 1.75
- ffn_shift: bfloat16 [768], P('fsdp'), may hold values from -1.1953125 to 1.1953125
Outputs:
- outputs: bfloat16 [256, 512, 768], P(('dp', 'fsdp'))
- input_grad: bfloat16 [256, 512, 768], P(('dp', 'fsdp'))
- qkv_weight_grad: float32 [768, 2304], P('fsdp')
- query_bias_grad: float32 [768], P('fsdp')
- value_bias_grad: float32 [768], P('fsdp')
- out_weight_grad: float32 [768, 768], P('fsdp')
- out_bias_grad: float32 [768], P('fsdp')
- attn_gain_grad: float32 [768], P('fsdp')
- attn_shift_grad: float32 [768], P('fsdp')
- up_weight_grad: float32 [768, 3072], P('fsdp')
- up_bias_grad: float32 [3072], P('fsdp')
- down_weight_grad: float32 [3072, 768], P('fsdp')
- down_bias_grad: float32 [768], P('fsdp')
- ffn_gain_grad: float32 [768], P('fsdp')
- ffn_shift_grad: float32 [768], P('fsdp')
Inputs may be any that keep to these rules, and one draw needn't show every extreme that they name: `segment_ids`: on every page the segment numbers never fall; each segment holds 1 to half of 512 tokens, one exactly that many.
All inputs are finite; a program needn't handle non-finite values.
Results may differ from a plain program's by a relative error of at most 0.022.
Values may be sent and summed in bfloat16 or wider, within the bound.
A program may use at most 128 MiB of HBM per device.

v0:
```python
import math

import jax
import jax.numpy as jnp
from jax import lax
from jax.sharding import PartitionSpec as P

HEADS = 12
HD = 64


def scaled_rows(values, gain):
    centre = jnp.mean(values, axis=-1, keepdims=True)
    centred = values - centre
    spread = jnp.mean(centred * centred, axis=-1, keepdims=True)
    return centred * lax.rsqrt(spread + 1e-12) * gain


def gelu_exact(values):
    return 0.5 * values * (1.0 + lax.erf(values * 0.7071067811865476))


def gelu_slope(values):
    return (
        0.5 * (1.0 + lax.erf(values * 0.7071067811865476))
        + values * jnp.exp(-0.5 * values * values) * 0.3989422804014327
    )


def head_columns(array, first_head, block_heads):
    return array[:, first_head * HD : (first_head + block_heads) * HD].reshape(
        array.shape[0], block_heads, HD
    )


def block_scores(query_part, key_part, same_segment):
    scores = jnp.einsum(
        "qhd,khd->hqk", query_part, key_part, preferred_element_type=jnp.float32
    ) * (1.0 / math.sqrt(HD))
    return jnp.where(same_segment[None], scores, -1e30)


def attend_forward(item):
    query_rows, key_rows, value_rows, segment_row = item
    length = query_rows.shape[0]
    same_segment = segment_row[:, None] == segment_row[None, :]
    block_heads = math.gcd(HEADS, 4)
    contexts = []
    summaries = []
    for first_head in range(0, HEADS, block_heads):
        query_part = head_columns(query_rows, first_head, block_heads)
        key_part = head_columns(key_rows, first_head, block_heads)
        value_part = head_columns(value_rows, first_head, block_heads)
        scores = block_scores(query_part, key_part, same_segment)
        row_peak = jnp.max(scores, axis=-1, keepdims=True)
        exp_terms = jnp.exp(scores - row_peak)
        row_total = jnp.sum(exp_terms, axis=-1, keepdims=True)
        weights_low = (exp_terms / row_total).astype(jnp.bfloat16)
        context = jnp.einsum(
            "hqk,khd->qhd", weights_low, value_part, preferred_element_type=jnp.float32
        )
        contexts.append(context.reshape(length, block_heads * HD))
        summaries.append((row_peak + jnp.log(row_total))[:, :, 0])
    return (
        jnp.concatenate(contexts, axis=1).astype(jnp.bfloat16),
        jnp.concatenate(summaries, axis=0),
    )


def attend_backward(item):
    query_rows, key_rows, value_rows, segment_row, summary, grad_context = item
    length = query_rows.shape[0]
    same_segment = segment_row[:, None] == segment_row[None, :]
    block_heads = math.gcd(HEADS, 4)
    score_scale = 1.0 / math.sqrt(HD)
    grads_query = []
    grads_key = []
    grads_value = []
    for first_head in range(0, HEADS, block_heads):
        query_part = head_columns(query_rows, first_head, block_heads)
        key_part = head_columns(key_rows, first_head, block_heads)
        value_part = head_columns(value_rows, first_head, block_heads)
        grad_part = head_columns(grad_context, first_head, block_heads)
        scores = block_scores(query_part, key_part, same_segment)
        softmax_weights = jnp.exp(
            scores - summary[first_head : first_head + block_heads][:, :, None]
        )
        weights_low = softmax_weights.astype(jnp.bfloat16)
        grad_value = jnp.einsum(
            "hqk,qhd->khd", weights_low, grad_part, preferred_element_type=jnp.float32
        )
        grad_weights = jnp.einsum(
            "qhd,khd->hqk", grad_part, value_part, preferred_element_type=jnp.float32
        )
        row_dot = jnp.sum(grad_weights * softmax_weights, axis=-1, keepdims=True)
        grad_scores = (softmax_weights * (grad_weights - row_dot)).astype(jnp.bfloat16)
        grad_query = (
            jnp.einsum("hqk,khd->qhd", grad_scores, key_part, preferred_element_type=jnp.float32)
            * score_scale
        )
        grad_key = (
            jnp.einsum("hqk,qhd->khd", grad_scores, query_part, preferred_element_type=jnp.float32)
            * score_scale
        )
        grads_query.append(grad_query.reshape(length, block_heads * HD))
        grads_key.append(grad_key.reshape(length, block_heads * HD))
        grads_value.append(grad_value.reshape(length, block_heads * HD))
    return jnp.concatenate(grads_query + grads_key + grads_value, axis=1).astype(jnp.bfloat16)


def body(
    inputs,
    segment_ids,
    cotangent,
    qkv_weight,
    query_bias,
    value_bias,
    out_weight,
    out_bias,
    attn_gain,
    attn_shift,
    up_weight,
    up_bias,
    down_weight,
    down_bias,
    ffn_gain,
    ffn_shift,
):
    (
        qkv_full,
        query_bias_full,
        value_bias_full,
        out_full,
        out_bias_full,
        attn_gain_full,
        attn_shift_full,
        up_full,
        up_bias_full,
        down_full,
        down_bias_full,
        ffn_gain_full,
        ffn_shift_full,
    ) = (
        lax.all_gather(qkv_weight, "fsdp", axis=0, tiled=True),
        lax.all_gather(query_bias, "fsdp", axis=0, tiled=True),
        lax.all_gather(value_bias, "fsdp", axis=0, tiled=True),
        lax.all_gather(out_weight, "fsdp", axis=0, tiled=True),
        lax.all_gather(out_bias, "fsdp", axis=0, tiled=True),
        lax.all_gather(attn_gain, "fsdp", axis=0, tiled=True),
        lax.all_gather(attn_shift, "fsdp", axis=0, tiled=True),
        lax.all_gather(up_weight, "fsdp", axis=0, tiled=True),
        lax.all_gather(up_bias, "fsdp", axis=0, tiled=True),
        lax.all_gather(down_weight, "fsdp", axis=0, tiled=True),
        lax.all_gather(down_bias, "fsdp", axis=0, tiled=True),
        lax.all_gather(ffn_gain, "fsdp", axis=0, tiled=True),
        lax.all_gather(ffn_shift, "fsdp", axis=0, tiled=True),
    )
    pages, length, width = inputs.shape
    tokens = pages * length
    flat_inputs = inputs.reshape(tokens, width)
    projected = jnp.dot(flat_inputs, qkv_full, preferred_element_type=jnp.float32)
    query_rows = (projected[:, :width] + query_bias_full.astype(jnp.float32)).astype(jnp.bfloat16)
    key_rows = projected[:, width : 2 * width].astype(jnp.bfloat16)
    value_rows = (projected[:, 2 * width :] + value_bias_full.astype(jnp.float32)).astype(
        jnp.bfloat16
    )
    query_pages = query_rows.reshape(pages, length, width)
    key_pages = key_rows.reshape(pages, length, width)
    value_pages = value_rows.reshape(pages, length, width)
    context, summary = lax.map(attend_forward, (query_pages, key_pages, value_pages, segment_ids))
    context_flat = context.reshape(tokens, width)
    attended = jnp.dot(
        context_flat, out_full, preferred_element_type=jnp.float32
    ) + out_bias_full.astype(jnp.float32)
    first_sum = flat_inputs.astype(jnp.float32) + attended
    first_norm = (
        scaled_rows(first_sum, attn_gain_full.astype(jnp.float32))
        + attn_shift_full.astype(jnp.float32)
    ).astype(jnp.bfloat16)
    ffn_inner = jnp.dot(
        first_norm, up_full, preferred_element_type=jnp.float32
    ) + up_bias_full.astype(jnp.float32)
    active = gelu_exact(ffn_inner).astype(jnp.bfloat16)
    branch = jnp.dot(active, down_full, preferred_element_type=jnp.float32) + down_bias_full.astype(
        jnp.float32
    )
    second_sum = first_norm.astype(jnp.float32) + branch
    outputs = scaled_rows(second_sum, ffn_gain_full.astype(jnp.float32)) + ffn_shift_full.astype(
        jnp.float32
    )
    qkv_back, out_back, up_back, down_back, attn_gain_back, ffn_gain_back = (
        lax.all_gather(qkv_weight, "fsdp", axis=0, tiled=True),
        lax.all_gather(out_weight, "fsdp", axis=0, tiled=True),
        lax.all_gather(up_weight, "fsdp", axis=0, tiled=True),
        lax.all_gather(down_weight, "fsdp", axis=0, tiled=True),
        lax.all_gather(attn_gain, "fsdp", axis=0, tiled=True),
        lax.all_gather(ffn_gain, "fsdp", axis=0, tiled=True),
    )
    grad_out = cotangent.reshape(tokens, width).astype(jnp.float32)
    second_value, second_pull = jax.vjp(scaled_rows, second_sum, ffn_gain_back.astype(jnp.float32))
    grad_second, grad_ffn_gain = second_pull(grad_out)
    grad_ffn_shift = jnp.sum(grad_out, axis=0)
    grad_branch = grad_second.astype(jnp.bfloat16)
    grad_down = jnp.einsum("tf,td->fd", active, grad_branch, preferred_element_type=jnp.float32)
    grad_down_bias = jnp.sum(grad_branch.astype(jnp.float32), axis=0)
    grad_active = jnp.einsum(
        "td,fd->tf", grad_branch, down_back, preferred_element_type=jnp.float32
    )
    grad_inner = (grad_active * gelu_slope(ffn_inner)).astype(jnp.bfloat16)
    grad_up = jnp.einsum("td,tf->df", first_norm, grad_inner, preferred_element_type=jnp.float32)
    grad_up_bias = jnp.sum(grad_inner.astype(jnp.float32), axis=0)
    grad_first = grad_second + jnp.einsum(
        "tf,df->td", grad_inner, up_back, preferred_element_type=jnp.float32
    )
    first_value, first_pull = jax.vjp(scaled_rows, first_sum, attn_gain_back.astype(jnp.float32))
    grad_first_sum, grad_attn_gain = first_pull(grad_first)
    grad_attn_shift = jnp.sum(grad_first, axis=0)
    grad_attended = grad_first_sum.astype(jnp.bfloat16)
    grad_out_weight = jnp.einsum(
        "td,te->de", context_flat, grad_attended, preferred_element_type=jnp.float32
    )
    grad_out_bias = jnp.sum(grad_attended.astype(jnp.float32), axis=0)
    grad_context = jnp.einsum(
        "te,de->td", grad_attended, out_back, preferred_element_type=jnp.float32
    ).astype(jnp.bfloat16)
    grad_mixed = lax.map(
        attend_backward,
        (
            query_pages,
            key_pages,
            value_pages,
            segment_ids,
            summary,
            grad_context.reshape(pages, length, width),
        ),
    )
    grad_mixed = grad_mixed.reshape(tokens, 3 * width)
    grad_qkv = jnp.einsum("td,te->de", flat_inputs, grad_mixed, preferred_element_type=jnp.float32)
    column_sums = jnp.sum(grad_mixed.astype(jnp.float32), axis=0)
    grad_query_bias = column_sums[:width]
    grad_value_bias = column_sums[2 * width :]
    input_grad = grad_first_sum + jnp.einsum(
        "te,de->td", grad_mixed, qkv_back, preferred_element_type=jnp.float32
    )
    local_grads = (
        grad_qkv,
        grad_query_bias,
        grad_value_bias,
        grad_out_weight,
        grad_out_bias,
        grad_attn_gain,
        grad_attn_shift,
        grad_up,
        grad_up_bias,
        grad_down,
        grad_down_bias,
        grad_ffn_gain,
        grad_ffn_shift,
    )
    shards = (
        lax.psum_scatter(local_grads[0], "fsdp", scatter_dimension=0, tiled=True),
        lax.psum_scatter(local_grads[1], "fsdp", scatter_dimension=0, tiled=True),
        lax.psum_scatter(local_grads[2], "fsdp", scatter_dimension=0, tiled=True),
        lax.psum_scatter(local_grads[3], "fsdp", scatter_dimension=0, tiled=True),
        lax.psum_scatter(local_grads[4], "fsdp", scatter_dimension=0, tiled=True),
        lax.psum_scatter(local_grads[5], "fsdp", scatter_dimension=0, tiled=True),
        lax.psum_scatter(local_grads[6], "fsdp", scatter_dimension=0, tiled=True),
        lax.psum_scatter(local_grads[7], "fsdp", scatter_dimension=0, tiled=True),
        lax.psum_scatter(local_grads[8], "fsdp", scatter_dimension=0, tiled=True),
        lax.psum_scatter(local_grads[9], "fsdp", scatter_dimension=0, tiled=True),
        lax.psum_scatter(local_grads[10], "fsdp", scatter_dimension=0, tiled=True),
        lax.psum_scatter(local_grads[11], "fsdp", scatter_dimension=0, tiled=True),
        lax.psum_scatter(local_grads[12], "fsdp", scatter_dimension=0, tiled=True),
    )
    totals = (
        lax.psum(shards[0].astype(jnp.bfloat16), "dp").astype(jnp.float32),
        lax.psum(shards[1].astype(jnp.bfloat16), "dp").astype(jnp.float32),
        lax.psum(shards[2].astype(jnp.bfloat16), "dp").astype(jnp.float32),
        lax.psum(shards[3].astype(jnp.bfloat16), "dp").astype(jnp.float32),
        lax.psum(shards[4].astype(jnp.bfloat16), "dp").astype(jnp.float32),
        lax.psum(shards[5].astype(jnp.bfloat16), "dp").astype(jnp.float32),
        lax.psum(shards[6].astype(jnp.bfloat16), "dp").astype(jnp.float32),
        lax.psum(shards[7].astype(jnp.bfloat16), "dp").astype(jnp.float32),
        lax.psum(shards[8].astype(jnp.bfloat16), "dp").astype(jnp.float32),
        lax.psum(shards[9].astype(jnp.bfloat16), "dp").astype(jnp.float32),
        lax.psum(shards[10].astype(jnp.bfloat16), "dp").astype(jnp.float32),
        lax.psum(shards[11].astype(jnp.bfloat16), "dp").astype(jnp.float32),
        lax.psum(shards[12].astype(jnp.bfloat16), "dp").astype(jnp.float32),
    )
    return (
        outputs.reshape(pages, length, width).astype(jnp.bfloat16),
        input_grad.reshape(pages, length, width).astype(jnp.bfloat16),
        totals[0],
        totals[1],
        totals[2],
        totals[3],
        totals[4],
        totals[5],
        totals[6],
        totals[7],
        totals[8],
        totals[9],
        totals[10],
        totals[11],
        totals[12],
    )


def solution(mesh):
    in_specs = (
        P(("dp", "fsdp"), None, None),
        P(("dp", "fsdp"), None),
        P(("dp", "fsdp"), None, None),
        P("fsdp", None),
        P("fsdp"),
        P("fsdp"),
        P("fsdp", None),
        P("fsdp"),
        P("fsdp"),
        P("fsdp"),
        P("fsdp", None),
        P("fsdp"),
        P("fsdp", None),
        P("fsdp"),
        P("fsdp"),
        P("fsdp"),
    )
    out_specs = (
        P(("dp", "fsdp"), None, None),
        P(("dp", "fsdp"), None, None),
        P("fsdp", None),
        P("fsdp"),
        P("fsdp"),
        P("fsdp", None),
        P("fsdp"),
        P("fsdp"),
        P("fsdp"),
        P("fsdp", None),
        P("fsdp"),
        P("fsdp", None),
        P("fsdp"),
        P("fsdp"),
        P("fsdp"),
    )
    return jax.shard_map(body, mesh=mesh, in_specs=in_specs, out_specs=out_specs, check_vma=False)
```

profile of v0, /device:TPU:1, one launch (start us, length us, event | category | flops | bytes accessed | tf_op | source)
XLA Modules:
  0.0 2147.7 jit_solution(7718725742867674907)
XLA Ops:
  23.4 262.1 %all-reduce.24 = (bf16[768]{0:T(1024)(128)(2,1)S(1)}, bf16[768]{0:T(1024)(128)(2,1)S(1)}, bf16[768]{0:T(1024)(128)(2,1)S(1)}, bf16[768]{0:T(1024)(128)(2,1)S(1)}...) all-reduce(bf16[768]{0:T(1024)(128)(2,1)S(1)} %dynamic-update-slice, ...), channel_id=1, replica_groups=mesh['dp'=4,'fsdp'=64] {'fsdp'}, use_global_device_ids=true, to_apply=%add.2 | all-reduce | flops 9216 | bytes 36864
  291.4 3.1 reshape.370
  294.5 280.4 %all-gather.10.cloned.1.call-done = bf16[64,12,2304]{2,1,0:T(8,128)(2,1)} async-done(((bf16[1,12,2304]{2,1,0:T(8,128)(2,1)}), bf16[64,12,2304]{2,1,0:T(8,128)(2,1)}) %all-gather.10.cloned.1.call-update) | async-done | bytes 3538960 | tf_op jit(solution)/shard_map/all_gather | solution.py:144
  574.9 4.9 reshape.368
  579.7 5.2 fusion.73
  591.3 2.1 fusion.32
  605.3 2.0 fusion.75
  620.7 262.0 %all-gather.14.cloned.1.call-done = bf16[64,12,3072]{2,1,0:T(8,128)(2,1)} async-done(((bf16[1,12,3072]{2,1,0:T(8,128)(2,1)}), bf16[64,12,3072]{2,1,0:T(8,128)(2,1)}) %all-gather.14.cloned.1.call-update) | async-done | bytes 4718608 | tf_op jit(solution)/shard_map/all_gather | solution.py:151
  882.7 8.0 reshape.372
  890.7 8.5 multiply_convert_fusion
  899.1 287.6 %all-gather.8.cloned.1.call-done = bf16[3072,768]{1,0:T(8,128)(2,1)} async-done(((bf16[48,768]{1,0:T(8,128)(2,1)}), bf16[3072,768]{1,0:T(8,128)(2,1)}) %all-gather.8.cloned.1.call-update) | async-done | bytes 4718608 | tf_op jit(solution)/shard_map/all_gather | solution.py:153
  1186.7 6.6 fusion.78
  1198.0 5.3 convert_reduce_fusion
  1203.3 4.8 multiply_reduce_fusion.3
  1208.1 5.5 fusion.79
  1213.7 5.3 fusion.80
  1219.6 3.6 fusion.63
  1223.9 2.3 convert_reduce_fusion.4
  1227.1 2.3 fusion.57
  1229.3 223.6 %fusion.62 = (f32[16,768]{1,0:T(8,128)}, f32[16,3072]{1,0:T(8,128)}) fusion(f32[768,768]{1,0:T(8,128)} %fusion.57, f32[768,3072]{1,0:T(8,128)} %fusion.79), kind=kCustom, calls=%all-reduce-scatter.2 | all-reduce-scatter fusion | flops 3932161 | bytes 12043264
  1463.3 2.3 convolution_convert_fusion
  1473.6 3.5 multiply_reduce_fusion.2
  1491.5 10.1 collective-permute-start.5
  1503.1 4.9 convolution_bitcast_fusion
  1508.0 3.6 collective-permute-start.7
  1511.6 2.2 collective-permute-start.8
  1513.9 2.1 collective-permute-start.9
  1516.0 4.0 collective-permute-start.10
  1521.8 2.2 collective-permute-start.12
  1524.1 3.4 collective-permute-start.13
  1533.4 4.6 collective-permute-start.17
  1538.0 2.5 collective-permute-start.18
  1540.5 2.3 collective-permute-start.19
  1542.8 2.8 collective-permute-start.20
  1546.4 4.0 collective-permute-start.21
  1550.4 324.1 %all-reduce.35 = (bf16[768,2304]{0,1:T(8,128)(2,1)}, bf16[768]{0:T(1024)(128)(2,1)}, bf16[768]{0:T(1024)(128)(2,1)}, bf16[768]{0:T(1024)(128)(2,1)}, bf16[768]{0...) all-reduce(f32[768,2304]{0,1:T(8,128)} %convolution_bitcast_fusion,, ...), channel_id=2, replica_groups=mesh['dp'=4,'fsdp'=64] {'fsdp'}, use_global_device_ids=true, to_apply=%region_17.18.clone | all-reduce | flops 1778688 | bytes 10672128
  1884.2 2.3 dynamic-slice_convert_fusion
  1897.7 24.3 %concatenate.14 = bf16[268,768]{1,0:T(8,128)(2,1)} concatenate(bf16[12,768]{1,0:T(8,128)(2,1)} %copy-done.37, bf16[16,768]{1,0:T(8,128)(2,1)} %copy-done.47, bf16[16,768]{1,0:T(8,128)(2,1)} %copy-done.46, bf16[16,768]{1,0:T(8,128)(2,1)} %copy-done.45, bf16[16,768]{1,0:T(8,128)(2,1)} %copy-done.44, bf16[16,768]{1,0:T(8,128)(2,1)} %copy-done.43, bf16[16,768]{1,0:T(8,128)(2,1)} %copy-done.42, ...), dimensions={0} | concatenate | bytes 847872
  1922.0 3.4 collective-permute-start.27
  1925.3 9.1 collective-permute-start.28
  1934.4 3.4 collective-permute-start.29
  1937.9 2.2 collective-permute-start.30
  1940.1 2.8 collective-permute-start.16
  1945.1 40.0 %concatenate.15 = bf16[268,3072]{1,0:T(8,128)(2,1)} concatenate(bf16[12,3072]{1,0:T(8,128)(2,1)} %copy-done.35, bf16[16,3072]{1,0:T(8,128)(2,1)} %collective-permute-done.30, bf16[16,3072]{1,0:T(8,128)(2,1)} %collective-permute-done.29, bf16[16,3072]{1,0:T(8,128)(2,1)} %collective-permute-done.28, bf16[16,3072]{1,0:T(8,128)(2,1)} %collective-permute-done.27, ...), dimensions={0} | concatenate | bytes 3391488
  1988.2 5.1 fusion.34
  1993.3 96.0 %all-reduce.32.cloned.1.call-done = (bf16[12,2304]{0,1:T(8,128)(2,1)}, bf16[12]{0:T(256)(128)(2,1)}, bf16[12]{0:T(256)(128)(2,1)}, bf16[12,768]{1,0:T(8,128)(2,1...) async-done(((bf16[12,2304]{0,1:T(8,128)(2,1)}, ...) | async-done | bytes 74032 | tf_op jit(solution)/shard_map/psum | solution.py:276
  2089.3 2.0 copy.117
  2103.1 34.4 %all-reduce.34.cloned.1.call-done = (bf16[12,3072]{1,0:T(8,128)(2,1)}, bf16[48,768]{1,0:T(8,128)(2,1)}) async-done(((bf16[12,3072]{1,0:T(8,128)(2,1)}, bf16[48,768]{1,0:T(8,128)(2,1)}), (bf16[12,3072]{1,0:T(8,128)(2,1)}, bf16[48,768]{1,0:T(8,128)(2,1)})) %all-reduce.34.cloned.1.call-update) | async-done | bytes 147472 | tf_op jit(solution)/shard_map/psum | solution.py:283
  (333 shorter events, 140.3 us)
Async XLA Ops:
  7.2 284.2 %all-gather.12.cloned.1.call-start = ((), (), s32[]{:S(2)}) async-start(), calls=%async_computation.4 | async-start | bytes 1597440 | tf_op jit(solution)/shard_map/all_gather | solution.py:147
  7.9 567.0 %all-gather.10.cloned.1.call-start = ((), (), s32[]{:S(2)}) async-start(), calls=%async_computation.3 | async-start | bytes 4792320 | tf_op jit(solution)/shard_map/all_gather | solution.py:144
  8.7 874.0 %all-gather.14.cloned.1.call-start = ((), (), s32[]{:S(2)}) async-start(), calls=%async_computation.5 | async-start | bytes 6389760 | tf_op jit(solution)/shard_map/all_gather | solution.py:151
  9.4 1177.3 %all-gather.8.cloned.1.call-start = ((), (), s32[]{:S(2)}) async-start(), calls=%async_computation.1 | async-start | bytes 4792320 | tf_op jit(solution)/shard_map/all_gather | solution.py:153
  10.0 1976.7 %reduce-scatter.7.cloned.1.call-start = ((), (), s32[]{:S(2)}) async-start(), calls=%async_computation.2 | async-start | bytes 9584640 | tf_op jit(solution)/shard_map/reduce_scatter | solution.py:270
  1223.8 865.4 %all-reduce.32.cloned.1.call-start = ((), (), s32[]{:S(2)}) async-start(), calls=%async_computation.6 | async-start | bytes 1238016 | tf_op jit(solution)/shard_map/psum | solution.py:276
  1455.7 45.8 %collective-permute-start.1 = (bf16[16,768]{1,0:T(8,128)(2,1)}, bf16[16,768]{1,0:T(8,128)(2,1)}, u32[]{:S(2)}, u32[]{:S(2)}) collective-permute-start(bf16[16,768]{1,0:T(8,128)(2,1)} %convert.150), channel_id=1, source_target_pairs={{0,2},{1,3},{2,4},{3,5},{4,6},{5,7},{6,8},{7,9},{8,10},{9,11},{10,... | collective-permute-start | bytes 73736
  1457.6 50.4 %collective-permute-start.2 = (bf16[16,768]{1,0:T(8,128)(2,1)}, bf16[16,768]{1,0:T(8,128)(2,1)}, u32[]{:S(2)}, u32[]{:S(2)}) collective-permute-start(bf16[16,768]{1,0:T(8,128)(2,1)} %convert.150), channel_id=1, source_target_pairs={{0,3},{1,4},{2,5},{3,6},{4,7},{5,8},{6,9},{7,10},{8,11},{9,12},{10... | collective-permute-start | bytes 73736
  1459.5 52.1 %collective-permute-start.3 = (bf16[16,768]{1,0:T(8,128)(2,1)}, bf16[16,768]{1,0:T(8,128)(2,1)}, u32[]{:S(2)}, u32[]{:S(2)}) collective-permute-start(bf16[16,768]{1,0:T(8,128)(2,1)} %convert.150), channel_id=1, source_target_pairs={{0,4},{1,5},{2,6},{3,7},{4,8},{5,9},{6,10},{7,11},{8,12},{9,13},{1... | collective-permute-start | bytes 73736
  1461.4 52.5 %collective-permute-start.4 = (bf16[16,768]{1,0:T(8,128)(2,1)}, bf16[16,768]{1,0:T(8,128)(2,1)}, u32[]{:S(2)}, u32[]{:S(2)}) collective-permute-start(bf16[16,768]{1,0:T(8,128)(2,1)} %convert.150), channel_id=1, source_target_pairs={{0,5},{1,6},{2,7},{3,8},{4,9},{5,10},{6,11},{7,12},{8,13},{9,14},{... | collective-permute-start | bytes 73736
  1471.9 19.5 collective-permute-start.15
  1491.4 30.0 %copy-start.6 = (bf16[512,2304]{0,1:T(8,128)(2,1)}, bf16[512,2304]{0,1:T(8,128)(2,1)S(1)}, u32[]{:S(2)}) copy-start(bf16[512,2304]{0,1:T(8,128)(2,1)S(1)} %constant_dynamic-update-slice_fusion) | copy-start | bytes 7077892
  1491.5 24.5 %collective-permute-start.5 = (bf16[16,768]{1,0:T(8,128)(2,1)}, bf16[16,768]{1,0:T(8,128)(2,1)S(1)}, u32[]{:S(2)}, u32[]{:S(2)}) collective-permute-start(bf16[16,768]{1,0:T(8,128)(2,1)} %convert.150), channel_id=1, source_target_pairs={{0,6},{1,7},{2,8},{3,9},{4,10},{5,11},{6,12},{7,13},{8,14},{9,15},... | collective-permute-start | bytes 73736
  1501.6 18.5 collective-permute-start.6
  1508.0 42.4 %copy-start.52 = (f32[768]{0:T(1024)S(1)}, f32[768]{0:T(1024)}, u32[]{:S(2)}) copy-start(f32[768]{0:T(1024)} %convert_reduce_fusion.2) | copy-start | bytes 9220
  1508.0 42.4 %copy-start.53 = (f32[768]{0:T(1024)S(1)}, f32[768]{0:T(1024)}, u32[]{:S(2)}) copy-start(f32[768]{0:T(1024)} %get-tuple-element.107) | copy-start | bytes 9220
  1508.0 42.4 %copy-start.54 = (f32[768]{0:T(1024)S(1)}, f32[768]{0:T(1024)}, u32[]{:S(2)}) copy-start(f32[768]{0:T(1024)} %get-tuple-element.146) | copy-start | bytes 9220
  1508.0 42.4 %copy-start.55 = (f32[768]{0:T(1024)S(1)}, f32[768]{0:T(1024)}, u32[]{:S(2)}) copy-start(f32[768]{0:T(1024)} %get-tuple-element.148) | copy-start | bytes 9220
  1508.0 13.8 collective-permute-start.7
  1511.6 12.4 collective-permute-start.8
  1513.9 13.7 collective-permute-start.9
  1516.0 29.6 %copy-start.38 = (bf16[16,768]{1,0:T(8,128)(2,1)}, bf16[16,768]{1,0:T(8,128)(2,1)S(1)}, u32[]{:S(2)}) copy-start(bf16[16,768]{1,0:T(8,128)(2,1)S(1)} %collective-permute-done.5) | copy-start | bytes 73732
  1516.0 12.8 collective-permute-start.10
  1520.1 25.6 %copy-start.39 = (bf16[16,768]{1,0:T(8,128)(2,1)}, bf16[16,768]{1,0:T(8,128)(2,1)S(1)}, u32[]{:S(2)}) copy-start(bf16[16,768]{1,0:T(8,128)(2,1)S(1)} %collective-permute-done.6) | copy-start | bytes 73732
  1520.1 10.7 collective-permute-start.11
  1521.8 23.8 %copy-start.40 = (bf16[16,768]{1,0:T(8,128)(2,1)}, bf16[16,768]{1,0:T(8,128)(2,1)S(1)}, u32[]{:S(2)}) copy-start(bf16[16,768]{1,0:T(8,128)(2,1)S(1)} %collective-permute-done.7) | copy-start | bytes 73732
  1521.8 11.6 collective-permute-start.12
  1524.1 13.9 collective-permute-start.13
  1527.6 13.0 collective-permute-start.14
  1528.9 13.9 collective-permute-start
  1530.8 14.8 collective-permute-start.31
  1533.4 341.2 %collective-permute-start.17 = (bf16[16,3072]{1,0:T(8,128)(2,1)}, bf16[16,3072]{1,0:T(8,128)(2,1)}, u32[]{:S(2)}, u32[]{:S(2)}) collective-permute-start(bf16[16,3072]{1,0:T(8,128)(2,1)} %convert.149), channel_id=1, source_target_pairs={{0,2},{1,3},{2,4},{3,5},{4,6},{5,7},{6,8},{7,9},{8,10},{9,11},{10,... | collective-permute-start | bytes 294920
  1538.0 338.5 %collective-permute-start.18 = (bf16[16,3072]{1,0:T(8,128)(2,1)}, bf16[16,3072]{1,0:T(8,128)(2,1)}, u32[]{:S(2)}, u32[]{:S(2)}) collective-permute-start(bf16[16,3072]{1,0:T(8,128)(2,1)} %convert.149), channel_id=1, source_target_pairs={{0,3},{1,4},{2,5},{3,6},{4,7},{5,8},{6,9},{7,10},{8,11},{9,12},{10... | collective-permute-start | bytes 294920
  1540.5 337.9 %collective-permute-start.19 = (bf16[16,3072]{1,0:T(8,128)(2,1)}, bf16[16,3072]{1,0:T(8,128)(2,1)}, u32[]{:S(2)}, u32[]{:S(2)}) collective-permute-start(bf16[16,3072]{1,0:T(8,128)(2,1)} %convert.149), channel_id=1, source_target_pairs={{0,4},{1,5},{2,6},{3,7},{4,8},{5,9},{6,10},{7,11},{8,12},{9,13},{1... | collective-permute-start | bytes 294920
  1542.8 337.5 %collective-permute-start.20 = (bf16[16,3072]{1,0:T(8,128)(2,1)}, bf16[16,3072]{1,0:T(8,128)(2,1)}, u32[]{:S(2)}, u32[]{:S(2)}) collective-permute-start(bf16[16,3072]{1,0:T(8,128)(2,1)} %convert.149), channel_id=1, source_target_pairs={{0,5},{1,6},{2,7},{3,8},{4,9},{5,10},{6,11},{7,12},{8,13},{9,14},{... | collective-permute-start | bytes 294920
  1546.4 335.9 %collective-permute-start.21 = (bf16[16,3072]{1,0:T(8,128)(2,1)}, bf16[16,3072]{1,0:T(8,128)(2,1)}, u32[]{:S(2)}, u32[]{:S(2)}) collective-permute-start(bf16[16,3072]{1,0:T(8,128)(2,1)} %convert.149), channel_id=1, source_target_pairs={{0,6},{1,7},{2,8},{3,9},{4,10},{5,11},{6,12},{7,13},{8,14},{9,15},... | collective-permute-start | bytes 294920
  1874.6 47.4 %collective-permute-start.22 = (bf16[16,3072]{1,0:T(8,128)(2,1)}, bf16[16,3072]{1,0:T(8,128)(2,1)}, u32[]{:S(2)}, u32[]{:S(2)}) collective-permute-start(bf16[16,3072]{1,0:T(8,128)(2,1)} %convert.149), channel_id=1, source_target_pairs={{0,7},{1,8},{2,9},{3,10},{4,11},{5,12},{6,13},{7,14},{8,15},{9,16}... | collective-permute-start | bytes 294920
  1876.5 48.9 %collective-permute-start.23 = (bf16[16,3072]{1,0:T(8,128)(2,1)}, bf16[16,3072]{1,0:T(8,128)(2,1)}, u32[]{:S(2)}, u32[]{:S(2)}) collective-permute-start(bf16[16,3072]{1,0:T(8,128)(2,1)} %convert.149), channel_id=1, source_target_pairs={{0,8},{1,9},{2,10},{3,11},{4,12},{5,13},{6,14},{7,15},{8,16},{9,17... | collective-permute-start | bytes 294920
  1878.4 56.0 %collective-permute-start.24 = (bf16[16,3072]{1,0:T(8,128)(2,1)}, bf16[16,3072]{1,0:T(8,128)(2,1)}, u32[]{:S(2)}, u32[]{:S(2)}) collective-permute-start(bf16[16,3072]{1,0:T(8,128)(2,1)} %convert.149), channel_id=1, source_target_pairs={{0,9},{1,10},{2,11},{3,12},{4,13},{5,14},{6,15},{7,16},{8,17},{9,1... | collective-permute-start | bytes 294920
  1880.3 57.6 %collective-permute-start.25 = (bf16[16,3072]{1,0:T(8,128)(2,1)}, bf16[16,3072]{1,0:T(8,128)(2,1)}, u32[]{:S(2)}, u32[]{:S(2)}) collective-permute-start(bf16[16,3072]{1,0:T(8,128)(2,1)} %convert.149), channel_id=1, source_target_pairs={{0,10},{1,11},{2,12},{3,13},{4,14},{5,15},{6,16},{7,17},{8,18},{9,... | collective-permute-start | bytes 294920
  1882.3 57.9 %collective-permute-start.26 = (bf16[16,3072]{1,0:T(8,128)(2,1)}, bf16[16,3072]{1,0:T(8,128)(2,1)}, u32[]{:S(2)}, u32[]{:S(2)}) collective-permute-start(bf16[16,3072]{1,0:T(8,128)(2,1)} %convert.149), channel_id=1, source_target_pairs={{0,11},{1,12},{2,13},{3,14},{4,15},{5,16},{6,17},{7,18},{8,19},{9,... | collective-permute-start | bytes 294920
  1922.0 66.3 %copy-start.60 = (f32[512]{0:T(512)S(1)}, f32[512]{0:T(512)}, u32[]{:S(2)}) copy-start(f32[512]{0:T(512)} %negate_multiply_fusion) | copy-start | bytes 6148
  1922.0 22.4 %collective-permute-start.27 = (bf16[16,3072]{1,0:T(8,128)(2,1)}, bf16[16,3072]{1,0:T(8,128)(2,1)}, u32[]{:S(2)}, u32[]{:S(2)}) collective-permute-start(bf16[16,3072]{1,0:T(8,128)(2,1)} %convert.149), channel_id=1, source_target_pairs={{0,12},{1,13},{2,14},{3,15},{4,16},{5,17},{6,18},{7,19},{8,20},{9,... | collective-permute-start | bytes 294920
  1925.3 19.0 collective-permute-start.28
  1934.4 10.0 collective-permute-start.29
  1937.9 6.5 collective-permute-start.30
  1940.1 5.0 collective-permute-start.16
  1944.3 193.2 %all-reduce.34.cloned.1.call-start = ((), (), s32[]{:S(2)}) async-start(), calls=%async_computation.7 | async-start | bytes 344064 | tf_op jit(solution)/shard_map/psum | solution.py:283
  (64 other events, 280.1 us)
Sparse Core Ops, SparseCore 0:
  9.8 259.1 all-gather.11
  270.8 304.0 all-gather.9
  576.7 305.9 all-gather.13
  884.3 302.3 all-gather.7
  1224.0 353.1 reduce-scatter.6
  1944.5 144.7 all-reduce.31
  2092.5 44.9 all-reduce.33
where the time goes:
time: 2160 us; the launch traced here: 2150 us
  waiting for transfers between devices  964 us (45%)
  blocking collectives  810 us (38%)
  local copies, waits for them, and re-layouts  144 us (7%)
  starting transfers between devices  91.2 us (4%)
  matrix products  74.4 us (3%)
  other arithmetic  46.3 us (2%)
    unnamed x3, blocking collectives  810 us
    all_gather x1, waiting for transfers between devices, body(): lax.all_gather(down_weight, 'fsdp', axis=0, tiled=True)  288 us
    all_gather x1, waiting for transfers between devices, body(): lax.all_gather(qkv_weight, 'fsdp', axis=0, tiled=True)  280 us
    all_gather x1, waiting for transfers between devices, body(): lax.all_gather(up_weight, 'fsdp', axis=0, tiled=True)  262 us
    unnamed x190, local copies, waits for them, and re-layouts  113 us
    psum x1, waiting for transfers between devices, body(): lax.psum(shards[0].astype(jnp.bfloat16), 'dp').astype(jnp.float32)  96 us
    unnamed x32, starting transfers between devices  90.9 us
  transfers between devices with their start and end apart: 39, of which 6 were waited for; matrix products, arithmetic and copies ran while one was open for 20% of the time, Pallas kernels for 0%

commit v1 on v0

v1 whole, which is shorter than its diff:
```python
import functools
import types

import jax
import jax.numpy as jnp
from jax import lax
from jax.experimental import pallas as pl
from jax.experimental.pallas import tpu as pltpu
from jax.sharding import PartitionSpec as P

T = 512
D = 768
FF = 3072
BF = jnp.bfloat16
F32 = jnp.float32
MESH = pl.DeviceIdType.MESH
BLOCK = (2, 4, 2, 4, 48, 256)

SCRATCH = (
    ("G", pltpu.VMEM((9,) + BLOCK, BF)),
    ("GV", pltpu.VMEM((2, 4, 2, 4, 16, 128), BF)),
    ("gr", pltpu.VMEM((4,) + BLOCK, BF)),
    ("rd", pltpu.VMEM((6, 4, 2, 4, 48, 256), BF)),
    ("r1", pltpu.VMEM((6, 3, 4, 2, 48, 256), BF)),
    ("r2", pltpu.VMEM((6, 7, 2, 48, 256), BF)),
    ("r3", pltpu.VMEM((6, 4, 48, 256), BF)),
    ("fin", pltpu.VMEM((9, 48, 256), F32)),
    ("qkv", pltpu.VMEM((3, 3, T, 256), BF)),
    ("p", pltpu.VMEM((12, T, T), BF)),
    ("mask", pltpu.VMEM((T, T), BF)),
    ("ctx", pltpu.VMEM((T, D), BF)),
    ("n1", pltpu.VMEM((T, D), F32)),
    ("rs1", pltpu.VMEM((T, 128), F32)),
    ("fn", pltpu.VMEM((T, D), BF)),
    ("act", pltpu.VMEM((4, 3 * T, 256), BF)),
    ("slope", pltpu.VMEM((4, T, D), BF)),
    ("acc", pltpu.VMEM((T, D), F32)),
    ("gb", pltpu.VMEM((T, D), BF)),
    ("tr", pltpu.VMEM((D, T), BF)),
    ("perm", pltpu.VMEM((192, 192), BF)),
    ("vec", pltpu.VMEM((16, D), F32)),
    ("ub", pltpu.VMEM((8, FF), F32)),
    ("vg", pltpu.VMEM((16, D), F32)),
    ("va", pltpu.VMEM((14, 8, D), F32)),
    ("vo", pltpu.VMEM((3, 8, D), F32)),
    ("small", pltpu.VMEM((16, 128), F32)),
    ("own", pltpu.VMEM((48, 256), F32)),
)
SEMS = (
    ("zs", (10, 7)), ("zr", (10, 4)), ("xs", (10, 3)), ("xr", (10, 3)),
    ("ys", (10, 2)), ("yr", (10, 2)), ("ds", (10,)), ("dr", (10,)),
    ("rds", (9,)), ("rdr", (9,)), ("p1s", (9, 3)), ("p1r", (9, 3)),
    ("p2s", (9, 4)), ("p2r", (9, 7)), ("p3s", (9, 4)), ("p3r", (9, 4)),
    ("fs", (9,)), ("fr", (9,)), ("vs", (15,)), ("vr", (15,)),
)
INS = (
    "x", "seg", "ct", "wqkv", "qb", "vb", "wout", "ob", "ag", "ash",
    "wup", "ub_in", "wdown", "db", "fg", "fsh",
)
OUTS = ("o_out", "o_ig", "o_qkv", "o_wout", "o_up", "o_down", "o_vec")


def dot(a, b):
    return lax.dot_general(a, b, (((1,), (0,)), ((), ())), preferred_element_type=F32)


def dot_nt(a, b):
    return lax.dot_general(a, b, (((1,), (1,)), ((), ())), preferred_element_type=F32)


def dot_tn(a, b):
    return lax.dot_general(a, b, (((0,), (0,)), ((), ())), preferred_element_type=F32)


def device(x, y, z, c):
    return ((y // 2) * 2 + c, z * 8 + lax.rem(y, 2) * 4 + x)


def kernel(*refs):
    names = INS + OUTS + tuple(n for n, _ in SCRATCH) + tuple(n for n, _ in SEMS) + ("ready",)
    s = types.SimpleNamespace(**dict(zip(names, refs, strict=True)))
    dp, fs = lax.axis_index("dp"), lax.axis_index("fsdp")
    C = lax.rem(dp, 2)
    YH = dp // 2
    Z = fs // 8
    YL = lax.rem(fs // 4, 2)
    X = lax.rem(fs, 4)
    Y = YH * 2 + YL
    ZT = Z // 4
    ZL = lax.rem(Z, 4)

    def copy(src, dst, send, recv, where):
        return pltpu.make_async_remote_copy(
            src_ref=src, dst_ref=dst, send_sem=send, recv_sem=recv, device_id=where, device_id_type=MESH
        )

    sibling = device(X, Y, Z, 1 - C)
    partners = (
        [sibling]
        + [device(lax.rem(X + d, 4), Y, Z, C) for d in (1, 2, 3)]
        + [device(X, lax.rem(Y + d, 4), Z, C) for d in (1, 2, 3)]
        + [device(X, Y, lax.rem(Z + d, 8), C) for d in range(1, 8)]
        + [device(lax.rem(X + d, 4), lax.rem(Y + 2, 4), Z, C) for d in (1, 2, 3)]
    )

    def greet(sem):
        for where in partners:
            pl.semaphore_signal(sem, inc=1, device_id=where, device_id_type=MESH)

    def gref(k):
        return s.GV if isinstance(k, int) and k == 9 else s.G.at[k]

    def z_copy(k, d):
        here = gref(k).at[ZT, ZL, YL, X]
        return copy(here, here, s.zs.at[k, d - 1], s.zr.at[k, ZL], device(X, Y, lax.rem(Z + d, 8), C))

    def z_recv(k, zl):
        here = gref(k).at[C, zl, YL, X]
        return copy(here, here, s.zs.at[k, 0], s.zr.at[k, zl], sibling)

    def x_copy(k, d):
        here = gref(k).at[C, :, YL, X]
        return copy(here, here, s.xs.at[k, d - 1], s.xr.at[k, d - 1], device(lax.rem(X + d, 4), Y, Z, C))

    def y_copy(k, i):
        here = gref(k).at[C, :, YL, pl.ds(2 * i, 2)]
        return copy(here, here, s.ys.at[k, i], s.yr.at[k, i], device(X, lax.rem(Y + 1 + 2 * i, 4), Z, C))

    def d_copy(k):
        here = gref(k).at[C]
        return copy(here, here, s.ds.at[k], s.dr.at[k], sibling)

    def ag_z(k):
        @pl.when(C == ZT)
        def _():
            for d in (4, 3, 5, 2, 6, 1, 7):
                z_copy(k, d).start()

    def ag_x(k):
        for zl in range(4):
            @pl.when(jnp.logical_or(C != ZT, zl != ZL))
            def _():
                z_recv(k, zl).wait_recv()
        for d in (2, 1, 3):
            x_copy(k, d).start()

    def ag_y(k):
        for d in (1, 2, 3):
            x_copy(k, d).wait_recv()
        for i in (0, 1):
            y_copy(k, i).start()

    def ag_d(k):
        for i in (0, 1):
            y_copy(k, i).wait_recv()
        d_copy(k).start()

    def ag_done(k):
        d_copy(k).wait()
        @pl.when(C == ZT)
        def _():
            for d in range(1, 8):
                z_copy(k, d).wait_send()
        for d in (1, 2, 3):
            x_copy(k, d).wait_send()
        for i in (0, 1):
            y_copy(k, i).wait_send()

    def ag_tick(t):
        for lag, step in ((2, ag_d), (1, ag_y), (0, ag_x)):
            i = t - lag
            if i == 0:
                step(9)
            if 0 <= i <= 8:
                step(i)

    def own_block(k, parts):
        for m, part in enumerate(parts):
            s.own[12 * m : 12 * m + 12, :] = part.astype(F32)
        s.G[k, ZT, ZL, YL, X] = s.own[...].astype(BF)

    for g in range(3):
        lo = 256 * g
        own_block(g, [s.wqkv[:, m * D + lo : m * D + lo + 256] for m in range(3)] + [s.wout[:, lo : lo + 256]])
    for g in range(3):
        lo = 256 * g
        own_block(3 + g, [s.wup[:, m * D + lo : m * D + lo + 256] for m in range(4)])
        s.G[6 + g, ZT, ZL, YL, X] = s.wdown[:, lo : lo + 256]
    s.small[...] = jnp.zeros((16, 128), F32)
    for i, v in enumerate((s.qb, s.vb, s.ob, s.ag, s.ash, s.db, s.fg, s.fsh)):
        s.small[i : i + 1, 0:12] = v[...].astype(F32)
    s.small[8:9, 0:48] = s.ub_in[...].astype(F32)
    s.GV[ZT, ZL, YL, X] = s.small[...].astype(BF)

    barrier = pltpu.get_barrier_semaphore()
    greet(barrier)
    pl.semaphore_wait(barrier, len(partners))

    ag_z(9)
    for k in range(9):
        ag_z(k)

    row = lax.broadcasted_iota(jnp.int32, (192, 192), 0)
    col = lax.broadcasted_iota(jnp.int32, (192, 192), 1)
    swapped = lax.rem(row // 12, 4) * 48 + (row // 48) * 12 + lax.rem(row, 12)
    s.perm[...] = (col == swapped).astype(F32).astype(BF)
    segf = jnp.broadcast_to(s.seg[...].astype(F32), (128, T))
    seg_col = jnp.transpose(segf)[:, 0:1]
    s.mask[...] = jnp.where(seg_col == segf[0:1, :], 0.0, -1e30).astype(BF)
    s.vg[...] = jnp.zeros((16, D), F32)

    def reorder(src, dst):
        @pl.loop(0, 16)
        def _(i):
            a, b, c = i // 8, lax.rem(i // 2, 4), lax.rem(i, 2)
            v = src[a, b, c].reshape(192, 256)
            w = dot(s.perm[...], v).astype(BF)
            dst[a, b, c] = w.reshape(4, 48, 256)

    def weight(k, m):
        return s.G[k, :, :, :, m].reshape(D, 256)

    def weight_row(base, m):
        return jnp.concatenate([weight(base + g, m) for g in range(3)], axis=1)

    def down_rows(m):
        parts = [s.G[6 + g, m // 2, pl.ds(2 * (m % 2), 2)].reshape(D, 256) for g in range(3)]
        return jnp.concatenate(parts, axis=1)

    def active(m):
        return jnp.concatenate([s.act[m, T * g : T * g + T] for g in range(3)], axis=1)

    ag_tick(0)
    ag_tick(1)
    ag_tick(2)
    ag_done(9)

    pick_r = lax.broadcasted_iota(jnp.int32, (128, D), 0)
    pick_c = lax.broadcasted_iota(jnp.int32, (128, D), 1)
    s.vec[...] = jnp.zeros((16, D), F32)
    s.ub[...] = jnp.zeros((8, FF), F32)

    @pl.loop(0, 8)
    def _(i):
        gv = s.GV[i // 4, lax.rem(i, 4)].reshape(128, 128)
        wide = dot(gv, (lax.rem(pick_c, 12) == pick_r).astype(F32).astype(BF))
        owner = lax.broadcasted_iota(jnp.int32, (128, D), 0) // 16 + 8 * i
        lane = lax.broadcasted_iota(jnp.int32, (128, D), 1) // 12
        s.vec[...] += jnp.sum(jnp.where(owner == lane, wide, 0.0).reshape(8, 16, D), axis=0)
        sel_r = lax.broadcasted_iota(jnp.int32, (8, 128), 0)
        sel_c = lax.broadcasted_iota(jnp.int32, (8, 128), 1)
        rows8 = dot((sel_c == 16 * sel_r + 8).astype(F32).astype(BF), gv).astype(BF)
        for m in range(4):
            up_c = pick_c + m * D
            wide_up = dot(rows8, (lax.rem(up_c, 48) == pick_r).astype(F32).astype(BF))
            own_r = lax.broadcasted_iota(jnp.int32, (8, D), 0) + 8 * i
            own_c = (lax.broadcasted_iota(jnp.int32, (8, D), 1) + m * D) // 48
            s.ub[:, m * D : m * D + D] += jnp.where(own_r == own_c, wide_up, 0.0)

    s.ub[0:1, :] = jnp.sum(s.ub[...], axis=0, keepdims=True)

    head_lane = lax.broadcasted_iota(jnp.int32, (1, 128), 1) // 64

    def head_only(v, h):
        return jnp.where(head_lane == h, v, jnp.zeros_like(v))

    for g in range(3):
        ag_done(g)
        reorder(s.G.at[g], s.G.at[g])
        ag_tick(3 + 2 * g)
        xv = s.x[...]
        for m in range(3):
            v = dot(xv, weight(g, m))
            if m != 1:
                i = 0 if m == 0 else 1
                v = v + s.vec[i : i + 1, 256 * g : 256 * g + 256]
            s.qkv[m, g] = v.astype(BF)
        ag_tick(4 + 2 * g)

        @pl.loop(0, 2)
        def _(j):
            lanes = pl.ds(pl.multiple_of(j * 128, 128), 128)
            q = s.qkv[0, g, :, lanes] * 0.125
            k = s.qkv[1, g, :, lanes]
            v = s.qkv[2, g, :, lanes]
            out = jnp.zeros((T, 128), F32)
            for h in range(2):
                sc = dot_nt(head_only(q, h), k) + s.mask[...].astype(F32)
                e = jnp.exp(sc - jnp.max(sc, axis=1, keepdims=True))
                w = (e * (1.0 / jnp.sum(e, axis=1, keepdims=True))).astype(BF)
                s.p[4 * g + 2 * j + h] = w
                out = out + dot(w, head_only(v, h))
            s.ctx[:, pl.ds(pl.multiple_of(g * 256 + j * 128, 128), 128)] = out.astype(BF)

    ag_tick(9)
    cv = s.ctx[...]
    for g in range(3):
        s.acc[:, 256 * g : 256 * g + 256] = dot(cv, weight(g, 3))
    ag_tick(10)

    @pl.loop(0, 16)
    def _(i):
        rows = pl.ds(pl.multiple_of(i * 32, 32), 32)
        v = s.acc[rows, :] + s.vec[2:3, :] + s.x[rows, :].astype(F32)
        v = v - jnp.mean(v, axis=1, keepdims=True)
        r = lax.rsqrt(jnp.mean(v * v, axis=1, keepdims=True) + 1e-12)
        n = v * r
        s.n1[rows, :] = n
        s.rs1[rows, :] = jnp.broadcast_to(r, (32, 128))
        s.fn[rows, :] = (n * s.vec[3:4, :] + s.vec[4:5, :]).astype(BF)

    fv = s.fn[...]
    for g in range(3):
        ag_done(3 + g)
        reorder(s.G.at[3 + g], s.G.at[3 + g])
        for m in range(4):
            lo = 256 * g
            u = dot(fv, weight(3 + g, m)) + s.ub[0:1, m * D + lo : m * D + lo + 256]
            half = 0.5 * (1.0 + lax.erf(u * 0.7071067811865476))
            s.act[m, T * g : T * g + T] = (u * half).astype(BF)
            s.slope[m, :, lo : lo + 256] = (half + u * jnp.exp(-0.5 * u * u) * 0.3989422804014327).astype(BF)
    for g in range(3):
        ag_done(6 + g)
        lo = 256 * g
        total = jnp.zeros((T, 256), F32)
        for m in range(4):
            total = total + dot(active(m), s.G[6 + g, m // 2, 2 * (m % 2) : 2 * (m % 2) + 2].reshape(D, 256))
        s.acc[:, lo : lo + 256] = total

    @pl.loop(0, 16)
    def _(i):
        rows = pl.ds(pl.multiple_of(i * 32, 32), 32)
        v = s.acc[rows, :] + s.vec[5:6, :] + s.fn[rows, :].astype(F32)
        v = v - jnp.mean(v, axis=1, keepdims=True)
        r = lax.rsqrt(jnp.mean(v * v, axis=1, keepdims=True) + 1e-12)
        n = v * r
        gain = s.vec[6:7, :]
        s.o_out[rows, :] = (n * gain + s.vec[7:8, :]).astype(BF)
        u = s.ct[rows, :].astype(F32)
        ug = u * gain
        un = u * n
        grad = r * (ug - jnp.mean(ug, axis=1, keepdims=True) - n * jnp.mean(ug * n, axis=1, keepdims=True))
        low = grad.astype(BF)
        s.acc[rows, :] = grad
        s.gb[rows, :] = low
        s.vg[5:6, :] += jnp.sum(low.astype(F32), axis=0, keepdims=True)
        s.vg[6:7, :] += jnp.sum(un, axis=0, keepdims=True)
        s.vg[7:8, :] += jnp.sum(u, axis=0, keepdims=True)

    def rd_copy(j):
        return copy(
            s.gr.at[j % 4, 1 - C], s.rd.at[j % 6], s.rds.at[j], s.rdr.at[j], sibling
        )

    def p1_copy(j, d, c):
        if c == 0:
            xx = lax.rem(X + d, 4)
            src, where = s.gr.at[j % 4, 0, :, :, xx], device(xx, Y, Z, 0)
        else:
            yy = lax.rem(Y + d, 4)
            src = s.gr.at[j % 4, 1, :, lax.rem(yy, 2), pl.ds(2 * (yy // 2), 2)]
            where = device(X, yy, Z, 1)
        return copy(src, s.r1.at[j % 6, d - 1], s.p1s.at[j, d - 1], s.p1r.at[j, d - 1], where)

    def p2_copy(j, zl):
        zz = C * 4 + zl
        slot = lax.rem(Z - zz + 8, 8) - 1
        return copy(
            s.r1.at[j % 6, 0, zl], s.r2.at[j % 6, slot], s.p2s.at[j, zl], s.p2r.at[j, slot],
            device(X, Y, zz, C),
        )

    def p2_recv(j, slot):
        return copy(
            s.r1.at[j % 6, 0, 0], s.r2.at[j % 6, slot], s.p2s.at[j, 0], s.p2r.at[j, slot], sibling
        )

    def p3_copy0(j, d):
        yy = lax.rem(Y + d, 4)
        return copy(
            s.r2.at[j % 6, 0, lax.rem(yy, 2)], s.r3.at[j % 6, Y], s.p3s.at[j, d], s.p3r.at[j, Y],
            device(X, yy, Z, 0),
        )

    def p3_copy1(j, i, other):
        xx = 2 * YH + i
        yy = lax.rem(Y + 2 * other, 4)
        return copy(
            s.r2.at[j % 6, 0, i], s.r3.at[j % 6, X], s.p3s.at[j, 2 * i + other], s.p3r.at[j, X],
            device(xx, yy, Z, 1),
        )

    def p3_recv(j, slot):
        return copy(
            s.r2.at[j % 6, 0, 0], s.r3.at[j % 6, slot], s.p3s.at[j, 0], s.p3r.at[j, slot], sibling
        )

    def f_copy(j):
        here = s.fin.at[j]
        return copy(here, here, s.fs.at[j], s.fr.at[j], sibling)

    def rs_d(j):
        rd_copy(j).start()

    def rs_p1(j):
        rd_copy(j).wait()

        @pl.loop(0, 8)
        def _(i):
            a, b = i // 2, lax.rem(i, 2)
            v = s.gr[j % 4, C, a, b].astype(F32) + s.rd[j % 6, a, b].astype(F32)
            s.gr[j % 4, C, a, b] = v.astype(BF)

        for c in (0, 1):
            @pl.when(C == c)
            def _():
                for d in (2, 1, 3):
                    p1_copy(j, d, c).start()

    def rs_p2(j):
        for c in (0, 1):
            @pl.when(C == c)
            def _():
                for d in (1, 2, 3):
                    p1_copy(j, d, c).wait()

        @pl.loop(0, 8)
        def _(i):
            a, b = i // 2, lax.rem(i, 2)
            mine = s.gr[j % 4, C, a, jnp.where(C == 0, b, YL), jnp.where(C == 0, X, 2 * YH + b)]
            v = mine.astype(F32)
            for d in range(3):
                v = v + s.r1[j % 6, d, a, b].astype(F32)
            s.r1[j % 6, 0, a, b] = v.astype(BF)

        for zl in range(4):
            @pl.when(C * 4 + zl != Z)
            def _():
                p2_copy(j, zl).start()

    def rs_p3(j):
        @pl.when(C == ZT)
        def _():
            for slot in range(7):
                p2_recv(j, slot).wait_recv()
            for b in range(2):
                v = s.r1[j % 6, 0, ZL, b].astype(F32)
                for slot in range(7):
                    v = v + s.r2[j % 6, slot, b].astype(F32)
                s.r2[j % 6, 0, b] = v.astype(BF)

        @pl.when(jnp.logical_and(C == 0, ZT == 0))
        def _():
            for d in (1, 2, 3):
                p3_copy0(j, d).start()

        @pl.when(jnp.logical_and(C == 1, ZT == 1))
        def _():
            for i in range(2):
                p3_copy1(j, i, 1).start()

                @pl.when(X != 2 * YH + i)
                def _():
                    p3_copy1(j, i, 0).start()

    def rs_f(j):
        own_slot = jnp.where(C == 0, Y, X)
        has_own = jnp.logical_or(C == 0, YH == X // 2)

        @pl.when(C == ZT)
        def _():
            @pl.when(has_own)
            def _():
                s.r3[j % 6, own_slot] = s.r2[j % 6, 0, jnp.where(C == 0, YL, lax.rem(X, 2))]
            for slot in range(4):
                @pl.when(jnp.logical_not(jnp.logical_and(has_own, own_slot == slot)))
                def _():
                    p3_recv(j, slot).wait_recv()
            v = s.r3[j % 6, 0].astype(F32)
            for slot in range(1, 4):
                v = v + s.r3[j % 6, slot].astype(F32)
            s.fin[j] = v
            f_copy(j).start()

    def rs_done(j):
        for zl in range(4):
            @pl.when(C * 4 + zl != Z)
            def _():
                p2_copy(j, zl).wait_send()

        @pl.when(jnp.logical_and(C == 0, ZT == 0))
        def _():
            for d in (1, 2, 3):
                p3_copy0(j, d).wait_send()

        @pl.when(jnp.logical_and(C == 1, ZT == 1))
        def _():
            for i in range(2):
                p3_copy1(j, i, 1).wait_send()

                @pl.when(X != 2 * YH + i)
                def _():
                    p3_copy1(j, i, 0).wait_send()

        @pl.when(C == ZT)
        def _():
            f_copy(j).wait_send()

        @pl.when(C != ZT)
        def _():
            f_copy(j).wait_recv()

    def rs_tick(t):
        for lag, step in ((4, rs_done), (3, rs_f), (2, rs_p3), (1, rs_p2), (0, rs_p1)):
            if 0 <= t - lag <= 5:
                step(t - lag)

    gbv = s.gb[...]
    for m in range(4):
        s.tr[...] = jnp.transpose(active(m))
        for g in range(3):
            v = dot(s.tr[...], gbv[:, 256 * g : 256 * g + 256])
            s.gr[g, m // 2, 2 * (m % 2) : 2 * (m % 2) + 2] = v.astype(BF).reshape(2, 2, 4, 48, 256)
    for g in range(3):
        rs_d(g)
    for m in range(4):
        low = (dot_nt(gbv, down_rows(m)) * s.slope[m].astype(F32)).astype(BF)
        s.slope[m] = low
        s.vg[8 + m : 9 + m, :] = jnp.sum(low.astype(F32), axis=0, keepdims=True)
    rs_tick(0)
    @pl.loop(0, 4)
    def _(m):
        s.acc[...] += dot_nt(s.slope[m], weight_row(3, m))

    rs_tick(1)
    s.tr[...] = jnp.transpose(s.fn[...])

    def up_chunk(g):
        for m in range(4):
            v = dot(s.tr[...], s.slope[m, :, 256 * g : 256 * g + 256])
            s.act[m, 0:D] = v.astype(BF)

    def put_chunk(slot):
        @pl.loop(0, 16)
        def _(i):
            a, b, c = i // 8, lax.rem(i // 2, 4), lax.rem(i, 2)
            v = s.act[:, pl.ds(pl.multiple_of(48 * i, 16), 48)].reshape(192, 256)
            s.gr[slot, a, b, c] = dot(s.perm[...], v).astype(BF).reshape(4, 48, 256)

    @pl.loop(0, 16)
    def _(i):
        rows = pl.ds(pl.multiple_of(i * 32, 32), 32)
        u = s.acc[rows, :]
        n = s.n1[rows, :]
        r = s.rs1[rows, 0:1]
        ug = u * s.vec[3:4, :]
        grad = r * (ug - jnp.mean(ug, axis=1, keepdims=True) - n * jnp.mean(ug * n, axis=1, keepdims=True))
        low = grad.astype(BF)
        s.acc[rows, :] = grad
        s.gb[rows, :] = low
        s.vg[2:3, :] += jnp.sum(low.astype(F32), axis=0, keepdims=True)
        s.vg[3:4, :] += jnp.sum(u * n, axis=0, keepdims=True)
        s.vg[4:5, :] += jnp.sum(u, axis=0, keepdims=True)

    for g in range(3):
        up_chunk(g)
        rs_tick(2 + g)
        put_chunk((3 + g) % 4)
        rs_d(3 + g)

    gav = s.gb[...]
    s.fn[...] = dot_nt(gav, weight_row(0, 3)).astype(BF)
    rs_tick(5)

    s.o_ig[...] = s.ctx[...]
    for g in range(3):
        @pl.loop(0, 2)
        def _(j):
            lanes = pl.ds(pl.multiple_of(j * 128, 128), 128)
            q = s.qkv[0, g, :, lanes]
            k = s.qkv[1, g, :, lanes]
            v = s.qkv[2, g, :, lanes]
            go = s.fn[:, pl.ds(pl.multiple_of(g * 256 + j * 128, 128), 128)]
            gq = jnp.zeros((T, 128), F32)
            gk = jnp.zeros((T, 128), F32)
            gvv = jnp.zeros((T, 128), F32)
            for h in range(2):
                goh = head_only(go, h)
                w = s.p[4 * g + 2 * j + h]
                wf = w.astype(F32)
                dw = dot_nt(goh, v)
                ds = (wf * (dw - jnp.sum(wf * dw, axis=1, keepdims=True))).astype(BF)
                gq = gq + dot(ds, head_only(k, h))
                gk = gk + dot_tn(ds, head_only(q, h))
                gvv = gvv + dot_tn(w, goh)
            s.qkv[0, g, :, lanes] = (gq * 0.125).astype(BF)
            s.qkv[1, g, :, lanes] = (gk * 0.125).astype(BF)
            s.qkv[2, g, :, lanes] = gvv.astype(BF)

        if g == 0:
            rs_tick(6)
            rs_tick(7)
            rs_tick(8)
            rs_tick(9)
            greet(s.ready)
            pl.semaphore_wait(s.ready, len(partners))
        s.tr[...] = jnp.transpose(s.o_ig[...])
        v = dot(s.tr[...], s.gb[:, 256 * g : 256 * g + 256])
        s.act[3, 0:D] = v.astype(BF)
        s.tr[...] = jnp.transpose(s.x[...])
        for m in range(3):
            s.act[m, 0:D] = dot(s.tr[...], s.qkv[m, g]).astype(BF)
        for i, m in ((0, 0), (1, 2)):
            s.vg[i : i + 1, 256 * g : 256 * g + 256] = jnp.sum(s.qkv[m, g].astype(F32), axis=0, keepdims=True)
        put_chunk((6 + g) % 4)
        rs_d(6 + g)
        if g >= 1:
            rs_p1(5 + g)

    @pl.loop(0, 3)
    def _(m):
        s.acc[...] += dot_nt(jnp.concatenate([s.qkv[m, g] for g in range(3)], axis=1), weight_row(0, m))

    s.o_ig[...] = s.acc[...].astype(BF)
    rs_p2(6)
    rs_p1(8)
    rs_p2(7)
    rs_p3(6)
    rs_p2(8)
    rs_p3(7)
    rs_f(6)
    rs_p3(8)
    rs_f(7)
    rs_f(8)
    for j in range(6, 9):
        rs_done(j)

    def v_copy(src, dst, i, where):
        return copy(src, dst, s.vs.at[i], s.vr.at[i], where)

    half = pl.ds(pl.multiple_of((1 - C) * 8, 8), 8)
    mine = pl.ds(pl.multiple_of(C * 8, 8), 8)
    first = v_copy(s.vg.at[half], s.va.at[13], 14, sibling)
    first.start()
    first.wait()
    s.vo[0] = s.vg[mine, :] + s.va[13]
    axes = (
        (0, [device(X, Y, lax.rem(Z + d, 8), C) for d in range(1, 8)]),
        (1, [device(lax.rem(X + d, 4), Y, Z, C) for d in (1, 2, 3)]),
        (0, [device(X, lax.rem(Y + d, 4), Z, C) for d in (1, 2, 3)]),
    )
    sem_at = 0
    for which, peers in axes:
        moves = []
        for i, where in enumerate(peers):
            moves.append(v_copy(s.vo.at[which], s.va.at[sem_at + i], sem_at + i, where))
        for c in moves:
            c.start()
        for c in moves:
            c.wait()
        v = s.vo[which]
        for i in range(len(peers)):
            v = v + s.va[sem_at + i]
        s.vo[1 - which] = v
        sem_at += len(peers)
    s.vg[mine, :] = s.vo[1]
    last = v_copy(s.vo.at[1], s.vo.at[2], 13, sibling)
    last.start()
    last.wait()
    s.vg[half, :] = s.vo[2]

    for g in range(3):
        lo = 256 * g
        v = s.fin[6 + g]
        for m in range(3):
            s.o_qkv[:, m * D + lo : m * D + lo + 256] = v[12 * m : 12 * m + 12]
        s.o_wout[:, lo : lo + 256] = v[36:48]
        v = s.fin[3 + g]
        for m in range(4):
            s.o_up[:, m * D + lo : m * D + lo + 256] = v[12 * m : 12 * m + 12]
        s.o_down[:, lo : lo + 256] = s.fin[g]
    vg = s.vg[...]
    lane_f = lax.broadcasted_iota(jnp.int32, (D, 128), 0)
    lane_r = lax.broadcasted_iota(jnp.int32, (D, 128), 1)
    pick = jnp.logical_and(lane_f - 12 * fs == lane_r, lane_r < 12).astype(F32)
    pick_up = jnp.logical_and(lane_f - 48 * lax.rem(fs, 16) == lane_r, lane_r < 48).astype(F32)
    exact = functools.partial(
        lax.dot_general, dimension_numbers=(((1,), (0,)), ((), ())), precision=lax.Precision.HIGHEST,
        preferred_element_type=F32,
    )
    thin = exact(vg, pick)
    thin_up = exact(vg, pick_up)
    quarter = fs // 16
    row_i = lax.broadcasted_iota(jnp.int32, (16, 128), 0)
    up_row = jnp.sum(jnp.where(row_i == 8 + quarter, thin_up, 0.0), axis=0, keepdims=True)
    s.o_vec[...] = jnp.where(row_i == 8, up_row, thin)


def body(
    inputs, segment_ids, cotangent, qkv_weight, query_bias, value_bias, out_weight, out_bias, attn_gain,
    attn_shift, up_weight, up_bias, down_weight, down_bias, ffn_gain, ffn_shift,
):
    row = lambda v: v.reshape(1, -1)
    vmem = pl.BlockSpec(memory_space=pltpu.VMEM)
    outs = pl.pallas_call(
        kernel,
        out_shape=(
            jax.ShapeDtypeStruct((T, D), BF),
            jax.ShapeDtypeStruct((T, D), BF),
            jax.ShapeDtypeStruct((12, 3 * D), F32),
            jax.ShapeDtypeStruct((12, D), F32),
            jax.ShapeDtypeStruct((12, FF), F32),
            jax.ShapeDtypeStruct((48, D), F32),
            jax.ShapeDtypeStruct((16, 128), F32),
        ),
        in_specs=[vmem] * len(INS),
        out_specs=(vmem,) * len(OUTS),
        scratch_shapes=[v for _, v in SCRATCH]
        + [pltpu.SemaphoreType.DMA(v) for _, v in SEMS]
        + [pltpu.SemaphoreType.REGULAR],
        compiler_params=pltpu.CompilerParams(
            collective_id=0, has_side_effects=True, vmem_limit_bytes=63 * 2**20
        ),
    )(
        inputs.reshape(T, D), segment_ids, cotangent.reshape(T, D), qkv_weight, row(query_bias),
        row(value_bias), out_weight, row(out_bias), row(attn_gain), row(attn_shift), up_weight,
        row(up_bias), down_weight, row(down_bias), row(ffn_gain), row(ffn_shift),
    )
    vec = outs[6]
    small = lambda i: vec[i, :12]
    return (
        outs[0].reshape(1, T, D), outs[1].reshape(1, T, D), outs[2], small(0), small(1), outs[3], small(2),
        small(3), small(4), outs[4], vec[8, :48], outs[5], small(5), small(6), small(7),
    )


def solution(mesh):
    pages = P(("dp", "fsdp"), None, None)
    mat = P("fsdp", None)
    v = P("fsdp")
    in_specs = (pages, P(("dp", "fsdp"), None), pages, mat, v, v, mat, v, v, v, mat, v, mat, v, v, v)
    out_specs = (pages, pages, mat, v, v, mat, v, v, v, mat, v, mat, v, v, v)
    return jax.shard_map(body, mesh=mesh, in_specs=in_specs, out_specs=out_specs, check_vma=False)
```

time: 2160 us -> 266 us (0.12)
  waiting for transfers between devices: 964 us -> 0 us
  blocking collectives: 810 us -> 0 us
  Pallas kernels: 0 us -> 252 us
  local copies, waits for them, and re-layouts: 144 us -> 8.93 us
  starting transfers between devices: 91.2 us -> 0 us
  matrix products: 74.4 us -> 0 us
  other arithmetic: 46.3 us -> 0 us
    all_gather x4 -> x0, waiting for transfers between devices: 830 us -> none  [the longest x1 288 us: body(): lax.all_gather(down_weight, 'fsdp', axis=0, tiled=True)]
    unnamed x3 -> x0, blocking collectives: 810 us -> none
    pallas_call x0 -> x1, Pallas kernels: none -> 252 us  [body(): pl.pallas_call(kernel, out_shape=(jax.ShapeDtypeStruct((T, D), BF), jax.S...]
    psum x2 -> x0, waiting for transfers between devices: 130 us -> none  [the longest x1 96 us: body(): lax.psum(shards[0].astype(jnp.bfloat16), 'dp').astype(jnp.float32)]
    unnamed x190 -> x16, local copies, waits for them, and re-layouts: 113 us -> 6.23 us
    unnamed x32 -> x0, starting transfers between devices: 90.9 us -> none
    dot_general x30 -> x0, matrix products: 74.4 us -> none  [the longest x1 8.47 us: body(): jnp.dot(first_norm, up_full, preferred_element_type=jnp.float32)]
    convert_element_type x26 -> x0, other arithmetic: 25.9 us -> none  [the longest x3 3.63 us: attend_backward(): (softmax_weights * (grad_weights - row_dot)).astype(jnp.bfloat16)]
  transfers between devices with their start and end apart: 39 -> 0, of which waited for: 6 -> 0; matrix products, arithmetic and copies ran while one was open for 20% -> 0% of each run, Pallas kernels for 0% -> 0%
where the time goes in v1:
time: 266 us; the launch traced here: 262 us
  Pallas kernels  252 us (95%)
  local copies, waits for them, and re-layouts  8.93 us (3%)
    pallas_call x1, Pallas kernels, body(): pl.pallas_call(kernel, out_shape=(jax.ShapeDtypeStruct((T, D), BF), jax.S...  252 us
    unnamed x16, local copies, waits for them, and re-layouts  6.23 us

profile of v1, /device:TPU:1, one launch (start us, length us, event | category | flops | bytes accessed | tf_op | source)
XLA Modules:
  0.0 261.9 jit_solution(2775966581764797962)
XLA Ops:
  0.7 252.1 %shard_map.271 = (bf16[512,768]{1,0:T(8,128)(2,1)}, bf16[512,768]{1,0:T(8,128)(2,1)}, f32[12,2304]{1,0:T(8,128)}, f32[12,768]{1,0:T(8,128)}, f32[12,3072]{1,0:T(...) custom-call(bf16[512,768]{1,0:T(8,128)(2,1)} %bitcast.31, s32[1,512]{1,0:T(1,128)} %refs_1_.1, bf16[512,768]{1,0:T(8,128)(2,1)} %bitcast.32, ...), custom_call_target="tpu_custom_call" | custom-call | tf_op jit(solution)/shard_map/pallas_call | solution.py:705
  252.7 1.5 slice_bitcast_fusion
  254.2 1.2 slice_bitcast_fusion.3
  255.4 0.0 copy-start
  255.4 2.1 copy.37
  257.6 0.0 copy-done
  257.6 0.0 copy-start.3
  257.6 0.9 copy.38
  258.5 0.1 copy-done.3
  258.6 0.0 copy-start.4
  258.6 0.0 copy-start.1
  258.6 0.7 copy.39
  259.3 0.1 copy-done.4
  259.4 0.6 copy.40
  260.0 0.0 copy-done.1
  260.0 0.0 copy-start.2
  260.0 0.7 copy.41
  260.7 0.3 copy-done.2
  261.0 0.7 copy.42
Async XLA Ops:
  255.4 2.1 copy-start
  257.6 1.0 copy-start.3
  258.6 0.8 copy-start.4
  258.6 1.4 copy-start.1
  260.0 1.0 copy-start.2
